TPU v7x, 32 devices: a whole 2x2x4 slice. The times are simulated.
32 devices in a mesh: grp: 2 (over y), ax: 8 (over z, x), ch: 2 (over core).
Axes of the slice: x: 2, y: 2, z: 4, core: 2. Of those that a mesh axis runs over, the one named last changes fastest.
Arguments:
- pair_first: bfloat16 [32, 16, 128], P(('grp', 'ax')), parts along dimension 0, may hold values from -6 to 6
- pair_second: bfloat16 [32, 16, 128], P(('grp', 'ax')), parts along dimension 0, may hold values from -6 to 6
- grad_out: bfloat16 [32, 16, 128], P(('grp', 'ax')), parts along dimension 0, may hold values from -6 to 6
- norm_gain: float32 [2, 128], replicated, may hold values from 0.1 to 1.9
- proj_weight: bfloat16 [2, 128, 512], replicated, may hold values from -0.5 to 0.5
- gate_weight: bfloat16 [2, 128, 128], replicated, may hold values from -0.5 to 0.5
- out_gain: float32 [2, 128], replicated, may hold values from 0.1 to 1.9
- out_weight: bfloat16 [2, 128, 128], replicated, may hold values from -0.5 to 0.5
Outputs:
- grad_in: bfloat16 [32, 16, 128], P(('grp', 'ax')), parts along dimension 0
- grad_proj: float32 [4, 128, 512], P('grp'), parts along dimension 0
- grad_gate: float32 [4, 128, 128], P('grp'), parts along dimension 0
- grad_out_weight: float32 [4, 128, 128], P('grp'), parts along dimension 0
There are 2 independent parts, one for each index of `grp`. A program takes and returns all parts, laid end to end along the dimension named above; an argument that names none is the same for every part. Nothing has to cross between parts.
All inputs are finite; a program needn't handle non-finite values.
Results may differ from a plain program's by a relative error of at most 0.017.
Values may be sent and summed in bfloat16 or wider, within the bound.
A program may use at most 128 MiB of HBM per device.

v0:
```python
import jax
import jax.numpy as jnp
from jax import lax
from jax.sharding import PartitionSpec as P

EPS = 1e-05


def normalize(values, axis):
    center = values - jnp.mean(values, axis=axis, keepdims=True)
    scale = lax.rsqrt(jnp.mean(center * center, axis=axis, keepdims=True) + EPS)
    return (center * scale, scale)


def norm_back(grad, normed, scale, axis):
    return scale * (
        grad
        - jnp.mean(grad, axis=axis, keepdims=True)
        - normed * jnp.mean(grad * normed, axis=axis, keepdims=True)
    )


def own_cells(values):
    share = values.shape[1] // lax.axis_size("ch")
    return lax.dynamic_slice_in_dim(values, lax.axis_index("ch") * share, share, 1)


def front(pair, layer_gain, w_proj, w_gate):
    width = w_proj.shape[1] // 4
    rows = pair.shape[0]
    count = pair.shape[1]
    pair_hat, pair_scale = normalize(pair.astype(jnp.float32), 2)
    flat_normed = (pair_hat * layer_gain).astype(jnp.bfloat16).reshape(-1, pair.shape[2])
    projected = jnp.dot(flat_normed, w_proj, preferred_element_type=jnp.float32)
    gate_sig = jax.nn.sigmoid(jnp.dot(flat_normed, w_gate, preferred_element_type=jnp.float32))
    sig_a = jax.nn.sigmoid(projected[:, width : 2 * width])
    sig_b = jax.nn.sigmoid(projected[:, 3 * width :])
    left_side = (
        (sig_a * projected[:, :width])
        .astype(jnp.bfloat16)
        .reshape(rows, count, width)
        .transpose(2, 0, 1)
    )
    right_side = (
        (sig_b * projected[:, 2 * width : 3 * width])
        .astype(jnp.bfloat16)
        .reshape(rows, count, width)
        .transpose(2, 0, 1)
    )
    left_half, right_half = (
        lax.all_to_all(left_side, "ch", split_axis=0, concat_axis=2, tiled=True),
        lax.all_to_all(right_side, "ch", split_axis=0, concat_axis=2, tiled=True),
    )
    return (pair_hat, pair_scale, flat_normed, projected, gate_sig, left_half, right_half)


def rear(tri_half, gate_sig, cotangent, layer_out_gain, w_out):
    tri = lax.all_to_all(
        tri_half.astype(jnp.bfloat16), "ch", split_axis=2, concat_axis=0, tiled=True
    ).astype(tri_half.dtype)
    tri_hat, tri_scale = normalize(tri, 0)
    tri_norm = (tri_hat * layer_out_gain[:, None, None]).astype(jnp.bfloat16)
    linear = jnp.einsum("cij,cd->ijd", tri_norm, w_out, preferred_element_type=jnp.float32).reshape(
        -1, w_out.shape[1]
    )
    flat_cot = cotangent.reshape(-1, cotangent.shape[2])
    d_linear = (flat_cot * gate_sig).astype(jnp.bfloat16)
    d_gate = (flat_cot * linear * gate_sig * (1.0 - gate_sig)).astype(jnp.bfloat16)
    d_cube = d_linear.reshape(cotangent.shape[0], cotangent.shape[1], -1)
    d_norm = jnp.einsum("ijd,cd->cij", d_cube, w_out, preferred_element_type=jnp.float32)
    g_out = jnp.einsum("cij,ijd->cd", tri_norm, d_cube, preferred_element_type=jnp.float32)
    tri_grad = norm_back(d_norm * layer_out_gain[:, None, None], tri_hat, tri_scale, 0).astype(
        jnp.bfloat16
    )
    grad_half = lax.all_to_all(tri_grad, "ch", split_axis=0, concat_axis=2, tiled=True)
    return (grad_half, d_gate, g_out)


def front_back(
    cotangent,
    left_half_grad,
    right_half_grad,
    pair_hat,
    pair_scale,
    flat_normed,
    projected,
    d_gate,
    layer_gain,
    w_proj,
    w_gate,
):
    d_left, d_right = (
        lax.all_to_all(
            left_half_grad.astype(jnp.bfloat16), "ch", split_axis=2, concat_axis=0, tiled=True
        ).astype(left_half_grad.dtype),
        lax.all_to_all(
            right_half_grad.astype(jnp.bfloat16), "ch", split_axis=2, concat_axis=0, tiled=True
        ).astype(right_half_grad.dtype),
    )
    width = d_left.shape[0]
    sig_a = jax.nn.sigmoid(projected[:, width : 2 * width])
    sig_b = jax.nn.sigmoid(projected[:, 3 * width :])
    flat_left = d_left.transpose(1, 2, 0).reshape(-1, width)
    flat_right = d_right.transpose(1, 2, 0).reshape(-1, width)
    d_proj = jnp.concatenate(
        [
            flat_left * sig_a,
            flat_left * projected[:, :width] * sig_a * (1.0 - sig_a),
            flat_right * sig_b,
            flat_right * projected[:, 2 * width : 3 * width] * sig_b * (1.0 - sig_b),
        ],
        axis=1,
    ).astype(jnp.bfloat16)
    d_normed = jnp.dot(d_proj, w_proj.T, preferred_element_type=jnp.float32) + jnp.dot(
        d_gate, w_gate.T, preferred_element_type=jnp.float32
    )
    g_proj = jnp.einsum("nc,nd->cd", flat_normed, d_proj, preferred_element_type=jnp.float32)
    g_gate = jnp.einsum("nc,nd->cd", flat_normed, d_gate, preferred_element_type=jnp.float32)
    d_pair = cotangent + norm_back(
        d_normed.reshape(cotangent.shape) * layer_gain, pair_hat, pair_scale, 2
    )
    return (d_pair, g_proj, g_gate)


def outgoing(pair, cotangent, layer_gain, w_proj, w_gate, layer_out_gain, w_out):
    pair_hat, pair_scale, flat_normed, projected, gate_sig, left_half, right_half = front(
        pair, layer_gain, w_proj, w_gate
    )
    tri_half = jnp.einsum(
        "cik,cjk->cij",
        left_half,
        lax.all_gather(right_half, "ax", axis=1, tiled=True),
        preferred_element_type=jnp.float32,
    )
    grad_half, d_gate, g_out = rear(tri_half, gate_sig, cotangent, layer_out_gain, w_out)
    d_left = jnp.einsum(
        "cij,cjk->cik",
        grad_half,
        lax.all_gather(right_half, "ax", axis=1, tiled=True),
        preferred_element_type=jnp.float32,
    )
    turned = lax.all_to_all(grad_half, "ax", split_axis=2, concat_axis=1, tiled=True)
    d_right = jnp.einsum(
        "cij,cik->cjk",
        turned,
        lax.all_gather(left_half, "ax", axis=1, tiled=True),
        preferred_element_type=jnp.float32,
    )
    d_pair, g_proj, g_gate = front_back(
        cotangent,
        d_left,
        d_right,
        pair_hat,
        pair_scale,
        flat_normed,
        projected,
        d_gate,
        layer_gain,
        w_proj,
        w_gate,
    )
    return (d_pair, g_proj, g_gate, g_out)


def incoming(pair, cotangent, layer_gain, w_proj, w_gate, layer_out_gain, w_out):
    pair_hat, pair_scale, flat_normed, projected, gate_sig, left_half, right_half = front(
        pair, layer_gain, w_proj, w_gate
    )
    turned = lax.all_to_all(left_half, "ax", split_axis=2, concat_axis=1, tiled=True)
    part = turned
    tri_half = jnp.einsum(
        "cki,ckj->cij",
        part,
        lax.all_gather(right_half, "ax", axis=1, tiled=True),
        preferred_element_type=jnp.float32,
    )
    grad_half, d_gate, g_out = rear(tri_half, gate_sig, cotangent, layer_out_gain, w_out)
    d_turned = jnp.einsum(
        "ckj,cij->cki",
        lax.all_gather(right_half, "ax", axis=1, tiled=True),
        grad_half,
        preferred_element_type=jnp.float32,
    )
    d_left = lax.all_to_all(
        d_turned.astype(jnp.bfloat16), "ax", split_axis=1, concat_axis=2, tiled=True
    ).astype(d_turned.dtype)
    part = left_half
    d_right = jnp.einsum(
        "cki,cij->ckj",
        part,
        lax.all_gather(grad_half, "ax", axis=1, tiled=True),
        preferred_element_type=jnp.float32,
    )
    d_pair, g_proj, g_gate = front_back(
        cotangent,
        d_left,
        d_right,
        pair_hat,
        pair_scale,
        flat_normed,
        projected,
        d_gate,
        layer_gain,
        w_proj,
        w_gate,
    )
    return (d_pair, g_proj, g_gate, g_out)


def on_device(
    pair_first, pair_second, grad_out, norm_gain, proj_weight, gate_weight, out_gain, out_weight
):
    count = pair_first.shape[1]
    second = incoming(
        own_cells(pair_second),
        own_cells(grad_out).astype(jnp.float32),
        norm_gain[1],
        proj_weight[1],
        gate_weight[1],
        out_gain[1],
        out_weight[1],
    )
    carried = lax.optimization_barrier(second[0].astype(jnp.bfloat16)).astype(jnp.float32)
    first = outgoing(
        own_cells(pair_first),
        carried,
        norm_gain[0],
        proj_weight[0],
        gate_weight[0],
        out_gain[0],
        out_weight[0],
    )
    totals = lax.psum(
        (
            jnp.stack([first[1], second[1]]),
            jnp.stack([first[2], second[2]]),
            jnp.stack([first[3], second[3]]),
        ),
        ("ax", "ch"),
    )
    grad_in = lax.all_gather(first[0].astype(jnp.bfloat16), "ch", axis=1, tiled=True)
    return (grad_in, totals[0] / count, totals[1] / count, totals[2] / count)


def solution(mesh):
    placed = (
        P(("grp", "ax"), None, None),
        P(("grp", "ax"), None, None),
        P(("grp", "ax"), None, None),
        P(),
        P(),
        P(),
        P(),
        P(),
    )
    return jax.shard_map(
        on_device,
        mesh=mesh,
        in_specs=placed,
        out_specs=(
            P(("grp", "ax"), None, None),
            P("grp", None, None),
            P("grp", None, None),
            P("grp", None, None),
        ),
        check_vma=False,
    )
```

profile of v0, /device:TPU:0, one launch (start us, length us, event | category | flops | bytes accessed | tf_op | source)
XLA Modules:
  0.0 325.5 jit_solution(17437239771286896225)
XLA Ops:
  11.5 3.2 all-to-all-start.9
  16.1 3.2 all-to-all-start.8
  19.5 32.3 %all_gather.19 = bf16[64,16,16]{0,2,1:T(8,128)(2,1)S(1)} all-gather(bf16[64,2,16]{0,2,1:T(8,128)(2,1)S(1)} %bitcast.373), channel_id=1, replica_groups=mesh['grp'=2,'ax'=8,'ch'=2] {'ax'}, dimensions={1}, use_global_device_ids=true | all-gather | bytes 36864 | tf_op jit(solution)/shard_map/all_gather | solution.py:132
  53.4 3.2 all-to-all-start.10
  57.1 30.5 %all_gather.20 = bf16[64,16,16]{0,2,1:T(8,128)(2,1)S(1)} all-gather(bf16[64,2,16]{0,2,1:T(8,128)(2,1)S(1)} %bitcast.365), channel_id=1, replica_groups=mesh['grp'=2,'ax'=8,'ch'=2] {'ax'}, dimensions={1}, use_global_device_ids=true | all-gather | bytes 36864 | tf_op jit(solution)/shard_map/all_gather | solution.py:146
  88.5 3.2 all-to-all-start.1
  93.5 3.2 all-to-all-start
  98.1 5.5 %all-to-all-start.2 = ((bf16[8,2,128]{2,1,0:T(2,128)(2,1)}), bf16[8,2,128]{2,1,0:T(2,128)(2,1)S(1)}, u32[]{:S(2)}, u32[]{:S(2)}) async-start(bf16[8,2,128]{2,1,0:T(2,128)(2,1)} %reshape.278), calls=%async_computation.2 | async-start | bytes 8192 | tf_op jit(solution)/shard_map/all_to_all | solution.py:169
  104.5 31.1 %all_gather.17 = bf16[64,16,16]{0,2,1:T(8,128)(2,1)S(1)} all-gather(bf16[64,2,16]{0,2,1:T(8,128)(2,1)S(1)} %bitcast.372), channel_id=1, replica_groups=mesh['grp'=2,'ax'=8,'ch'=2] {'ax'}, dimensions={1}, use_global_device_ids=true | all-gather | bytes 36864 | tf_op jit(solution)/shard_map/all_gather | solution.py:180
  137.1 3.8 %all_to_all.216 = bf16[2,2,512]{2,1,0:T(2,128)(2,1)S(1)} all-to-all(bf16[2,2,512]{2,1,0:T(2,128)(2,1)S(1)} %reshape.282), channel_id=1, replica_groups=mesh['grp'=2,'ax'=8,'ch'=2] {'ch'}, dimensions={0} | all-to-all | bytes 8192 | tf_op jit(solution)/shard_map/all_to_all | solution.py:58
  142.2 3.7 %all_to_all.217 = bf16[2,2,512]{2,1,0:T(2,128)(2,1)S(1)} all-to-all(bf16[2,2,512]{2,1,0:T(2,128)(2,1)S(1)} %reshape.284), channel_id=1, replica_groups=mesh['grp'=2,'ax'=8,'ch'=2] {'ch'}, dimensions={0} | all-to-all | bytes 8192 | tf_op jit(solution)/shard_map/all_to_all | solution.py:75
  146.2 30.5 %all_gather.18 = bf16[64,16,16]{0,2,1:T(8,128)(2,1)S(1)} all-gather(bf16[64,2,16]{0,2,1:T(8,128)(2,1)S(1)} %bitcast.367), channel_id=1, replica_groups=mesh['grp'=2,'ax'=8,'ch'=2] {'ax'}, dimensions={1}, use_global_device_ids=true | all-gather | bytes 36864 | tf_op jit(solution)/shard_map/all_gather | solution.py:191
  178.7 3.7 %all_to_all.218 = bf16[2,2,512]{2,1,0:T(2,128)(2,1)S(1)} all-to-all(bf16[2,2,512]{2,1,0:T(2,128)(2,1)S(1)} %reshape.286), channel_id=1, replica_groups=mesh['grp'=2,'ax'=8,'ch'=2] {'ch'}, dimensions={0} | all-to-all | bytes 8192 | tf_op jit(solution)/shard_map/all_to_all | solution.py:96
  182.4 5.4 %all-to-all-start.5 = ((bf16[8,2,128]{2,1,0:T(2,128)(2,1)}), bf16[8,2,128]{2,1,0:T(2,128)(2,1)S(1)}, u32[]{:S(2)}, u32[]{:S(2)}) async-start(bf16[8,2,128]{2,1,0:T(2,128)(2,1)} %reshape.288), calls=%async_computation.5 | async-start | bytes 8192 | tf_op jit(solution)/shard_map/all_to_all | solution.py:184
  188.2 6.0 %all-to-all-done.5 = bf16[8,2,128]{2,1,0:T(2,128)(2,1)S(1)} async-done(((bf16[8,2,128]{2,1,0:T(2,128)(2,1)}), bf16[8,2,128]{2,1,0:T(2,128)(2,1)S(1)}, u32[]{:S(2)}, u32[]{:S(2)}) %all-to-all-start.5) | async-done | bytes 4128 | tf_op jit(solution)/shard_map/all_to_all | solution.py:184
  194.4 3.7 %all_to_all.219 = bf16[2,2,512]{2,1,0:T(2,128)(2,1)S(1)} all-to-all(bf16[2,2,512]{2,1,0:T(2,128)(2,1)S(1)} %reshape.290), channel_id=1, replica_groups=mesh['grp'=2,'ax'=8,'ch'=2] {'ch'}, dimensions={0} | all-to-all | bytes 8192 | tf_op jit(solution)/shard_map/all_to_all | solution.py:93
  199.8 3.7 %all_to_all.220 = bf16[2,2,512]{2,1,0:T(2,128)(2,1)S(1)} all-to-all(bf16[2,2,512]{2,1,0:T(2,128)(2,1)S(1)} %reshape.298), channel_id=1, replica_groups=mesh['grp'=2,'ax'=8,'ch'=2] {'ch'}, dimensions={0} | all-to-all | bytes 8192 | tf_op jit(solution)/shard_map/all_to_all | solution.py:75
  205.1 3.7 %all_to_all.221 = bf16[2,2,512]{2,1,0:T(2,128)(2,1)S(1)} all-to-all(bf16[2,2,512]{2,1,0:T(2,128)(2,1)S(1)} %reshape.304), channel_id=1, replica_groups=mesh['grp'=2,'ax'=8,'ch'=2] {'ch'}, dimensions={0} | all-to-all | bytes 8192 | tf_op jit(solution)/shard_map/all_to_all | solution.py:93
  208.8 3.3 %all-to-all-start.13 = ((bf16[8,2,128]{2,1,0:T(2,128)(2,1)}), bf16[8,2,128]{2,1,0:T(2,128)(2,1)S(1)}, u32[]{:S(2)}, u32[]{:S(2)}) async-start(bf16[8,2,128]{2,1,0:T(2,128)(2,1)} %reshape.300), calls=%async_computation.13 | async-start | bytes 8192 | tf_op jit(solution)/shard_map/all_to_all | solution.py:142
  214.1 4.4 %all-to-all-done.13 = bf16[8,2,128]{2,1,0:T(2,128)(2,1)S(1)} async-done(((bf16[8,2,128]{2,1,0:T(2,128)(2,1)}), bf16[8,2,128]{2,1,0:T(2,128)(2,1)S(1)}, u32[]{:S(2)}, u32[]{:S(2)}) %all-to-all-start.13) | async-done | bytes 4128 | tf_op jit(solution)/shard_map/all_to_all | solution.py:142
  219.0 3.7 %all_to_all.222 = bf16[2,2,512]{2,1,0:T(2,128)(2,1)S(1)} all-to-all(bf16[2,2,512]{2,1,0:T(2,128)(2,1)S(1)} %reshape.302), channel_id=1, replica_groups=mesh['grp'=2,'ax'=8,'ch'=2] {'ch'}, dimensions={0} | all-to-all | bytes 8192 | tf_op jit(solution)/shard_map/all_to_all | solution.py:96
  224.7 1.8 all_gather.21
  226.5 88.0 %all-reduce.3.cloned.1.call-done = (f32[2,128,512]{2,1,0:T(8,128)}, f32[2,128,128]{2,1,0:T(8,128)}, f32[2,128,128]{2,1,0:T(8,128)}) async-done(((f32[2,128,512]{2,1,0:T(8,128)}, f32[2,128,128]{2,1,0:T(8,128)}, f32[2,128,128]{2,1,0:T(8,128)}), (f32[2,128,512]{2,1,0:T(8,128)}, f32[2,128,128]{2,1,0:T(8,128)}, f32[2,128,128]{2,1,0:T(8,128)})) %all-reduce.3.cloned.1.call-update) | async-done | bytes 786448 | tf_op jit(solution)/shard_map/psum | solution.py:233
  314.5 1.9 broadcast_multiply_fusion
  (191 shorter events, 28.3 us)
Async XLA Ops:
  7.2 0.7 copy-start.4
  7.9 0.7 copy-start.3
  8.8 0.7 copy-start.7
  11.5 4.6 %all-to-all-start.9 = ((bf16[2,2,512]{2,1,0:T(2,128)(2,1)}), bf16[2,2,512]{2,1,0:T(2,128)(2,1)S(1)}, u32[]{:S(2)}, u32[]{:S(2)}) async-start(bf16[2,2,512]{2,1,0:T(2,128)(2,1)} %reshape.294), calls=%async_computation.9 | async-start | bytes 8192 | tf_op jit(solution)/shard_map/all_to_all | solution.py:52
  16.1 35.7 %all-to-all-start.8 = ((bf16[2,2,512]{2,1,0:T(2,128)(2,1)}), bf16[2,2,512]{2,1,0:T(2,128)(2,1)S(1)}, u32[]{:S(2)}, u32[]{:S(2)}) async-start(bf16[2,2,512]{2,1,0:T(2,128)(2,1)} %reshape.292), calls=%async_computation.8 | async-start | bytes 8192 | tf_op jit(solution)/shard_map/all_to_all | solution.py:51
  52.4 4.3 %copy-start.9 = (bf16[2,128,128]{2,1,0:T(8,128)(2,1)S(1)}, bf16[2,128,128]{2,1,0:T(8,128)(2,1)}, u32[]{:S(2)}) copy-start(bf16[2,128,128]{2,1,0:T(8,128)(2,1)} %param.13) | copy-start | bytes 196612
  52.4 4.6 %copy-start = (bf16[2,128,512]{2,1,0:T(8,128)(2,1)S(1)}, bf16[2,128,512]{2,1,0:T(8,128)(2,1)}, u32[]{:S(2)}) copy-start(bf16[2,128,512]{2,1,0:T(8,128)(2,1)} %param.12) | copy-start | bytes 786436
  53.4 35.0 %all-to-all-start.10 = ((bf16[2,2,512]{2,1,0:T(2,128)(2,1)}), bf16[2,2,512]{2,1,0:T(2,128)(2,1)S(1)}, u32[]{:S(2)}, u32[]{:S(2)}) async-start(bf16[2,2,512]{2,1,0:T(2,128)(2,1)} %reshape.296), calls=%async_computation.10 | async-start | bytes 8192 | tf_op jit(solution)/shard_map/all_to_all | solution.py:58
  88.5 5.0 %all-to-all-start.1 = ((bf16[2,2,512]{2,1,0:T(2,128)(2,1)}), bf16[2,2,512]{2,1,0:T(2,128)(2,1)S(1)}, u32[]{:S(2)}, u32[]{:S(2)}) async-start(bf16[2,2,512]{2,1,0:T(2,128)(2,1)} %reshape.276), calls=%async_computation.1 | async-start | bytes 8192 | tf_op jit(solution)/shard_map/all_to_all | solution.py:51
  91.9 0.7 copy-start.6
  93.5 4.6 %all-to-all-start = ((bf16[2,2,512]{2,1,0:T(2,128)(2,1)}), bf16[2,2,512]{2,1,0:T(2,128)(2,1)S(1)}, u32[]{:S(2)}, u32[]{:S(2)}) async-start(bf16[2,2,512]{2,1,0:T(2,128)(2,1)} %reshape.280), calls=%async_computation | async-start | bytes 8192 | tf_op jit(solution)/shard_map/all_to_all | solution.py:52
  98.1 38.4 %all-to-all-start.2 = ((bf16[8,2,128]{2,1,0:T(2,128)(2,1)}), bf16[8,2,128]{2,1,0:T(2,128)(2,1)S(1)}, u32[]{:S(2)}, u32[]{:S(2)}) async-start(bf16[8,2,128]{2,1,0:T(2,128)(2,1)} %reshape.278), calls=%async_computation.2 | async-start | bytes 8192 | tf_op jit(solution)/shard_map/all_to_all | solution.py:169
  103.7 0.7 copy-start.5
  137.1 4.3 %copy-start.8 = (bf16[2,128,128]{2,1,0:T(8,128)(2,1)S(1)}, bf16[2,128,128]{2,1,0:T(8,128)(2,1)}, u32[]{:S(2)}) copy-start(bf16[2,128,128]{2,1,0:T(8,128)(2,1)} %param.15) | copy-start | bytes 196612
  182.4 11.8 %all-to-all-start.5 = ((bf16[8,2,128]{2,1,0:T(2,128)(2,1)}), bf16[8,2,128]{2,1,0:T(2,128)(2,1)S(1)}, u32[]{:S(2)}, u32[]{:S(2)}) async-start(bf16[8,2,128]{2,1,0:T(2,128)(2,1)} %reshape.288), calls=%async_computation.5 | async-start | bytes 8192 | tf_op jit(solution)/shard_map/all_to_all | solution.py:184
  208.8 9.6 %all-to-all-start.13 = ((bf16[8,2,128]{2,1,0:T(2,128)(2,1)}), bf16[8,2,128]{2,1,0:T(2,128)(2,1)S(1)}, u32[]{:S(2)}, u32[]{:S(2)}) async-start(bf16[8,2,128]{2,1,0:T(2,128)(2,1)} %reshape.300), calls=%async_computation.13 | async-start | bytes 8192 | tf_op jit(solution)/shard_map/all_to_all | solution.py:142
  212.1 102.4 %all-reduce.3.cloned.1.call-start = ((), (), s32[]{:S(2)}) async-start(), calls=%async_computation.15 | async-start | bytes 1572864 | tf_op jit(solution)/shard_map/psum | solution.py:233
  314.5 1.9 copy-start.2
  316.4 1.0 copy-start.1
Sparse Core Ops, SparseCore 0:
  224.7 89.7 all-reduce.2
where the time goes:
time: 327 us; the launch traced here: 325 us
  blocking collectives  152 us (46%)
  waiting for transfers between devices  99.4 us (30%)
  starting transfers between devices  30.3 us (9%)
  local copies, waits for them, and re-layouts  16.3 us (5%)
  between operations  14.5 us (4%)
  other arithmetic  7.43 us (2%)
  matrix products  5.5 us (2%)
    psum x1, waiting for transfers between devices, on_device(): lax.psum((jnp.stack([first[1], second[1]]), jnp.stack([first[2], second[2...  88 us
    all_gather x1, blocking collectives, outgoing(): lax.all_gather(right_half, 'ax', axis=1, tiled=True)  32.3 us
    all_gather x1, blocking collectives, incoming(): lax.all_gather(right_half, 'ax', axis=1, tiled=True)  31.1 us
    all_gather x1, blocking collectives, incoming(): lax.all_gather(grad_half, 'ax', axis=1, tiled=True)  30.5 us
    all_gather x1, blocking collectives, outgoing(): lax.all_gather(left_half, 'ax', axis=1, tiled=True)  30.5 us
    unnamed x51, local copies, waits for them, and re-layouts  11.7 us
    all_to_all x2, blocking collectives, front_back(): lax.all_to_all(right_half_grad.astype(jnp.bfloat16), 'ch', split_axis=2,...  7.38 us
    all_to_all x2, blocking collectives, rear(): lax.all_to_all(tri_grad, 'ch', split_axis=0, concat_axis=2, tiled=True)  7.38 us
  transfers between devices with their start and end apart: 9, of which 5 were waited for; matrix products, arithmetic and copies ran while one was open for 2% of the time, Pallas kernels for 0%

commit v1 on v0

--- a/solution.py
+++ b/solution.py
@@ -1,6 +1,10 @@
+import functools
+
 import jax
 import jax.numpy as jnp
 from jax import lax
+from jax.experimental import pallas as pl
+from jax.experimental.pallas import tpu as pltpu
 from jax.sharding import PartitionSpec as P
 
 EPS = 1e-05
@@ -207,7 +211,7 @@
     return (d_pair, g_proj, g_gate, g_out)
 
 
-def on_device(
+def split_crop(
     pair_first, pair_second, grad_out, norm_gain, proj_weight, gate_weight, out_gain, out_weight
 ):
     count = pair_first.shape[1]
@@ -242,6 +246,249 @@
     return (grad_in, totals[0] / count, totals[1] / count, totals[2] / count)
 
 
+def nt_dot(a, b):
+    return lax.dot_general(a, b, (((1,), (1,)), ((), ())), preferred_element_type=jnp.float32)
+
+
+def tn_dot(a, b):
+    return lax.dot_general(a, b, (((0,), (0,)), ((), ())), preferred_element_type=jnp.float32)
+
+
+def gather_kernel(shares, first_ref, second_ref, cot_ref, held, send_sem, recv_sem):
+    me = lax.axis_index("ax")
+    barrier = pltpu.get_barrier_semaphore()
+    for step in range(1, shares):
+        peer = lax.rem(me + step, shares)
+        pl.semaphore_signal(
+            barrier, inc=1, device_id={"ax": peer}, device_id_type=pl.DeviceIdType.MESH
+        )
+    held[me, 0] = second_ref[...]
+    held[me, 1] = cot_ref[...]
+    held[me, 2] = first_ref[...]
+    pl.semaphore_wait(barrier, shares - 1)
+    copies = []
+    for step in range(1, shares):
+        peer = lax.rem(me + step, shares)
+        copy = pltpu.make_async_remote_copy(
+            src_ref=held.at[me],
+            dst_ref=held.at[me],
+            send_sem=send_sem.at[step],
+            recv_sem=recv_sem.at[step],
+            device_id={"ax": peer},
+            device_id_type=pl.DeviceIdType.MESH,
+        )
+        copy.start()
+        copies.append(copy)
+    for copy in copies:
+        copy.wait()
+
+
+def gather_rows(first, second, cot, shares):
+    return pl.pallas_call(
+        functools.partial(gather_kernel, shares),
+        out_shape=jax.ShapeDtypeStruct((shares, 3) + first.shape, first.dtype),
+        in_specs=[pl.BlockSpec(memory_space=pltpu.VMEM)] * 3,
+        out_specs=pl.BlockSpec(memory_space=pltpu.VMEM),
+        scratch_shapes=[
+            pltpu.SemaphoreType.DMA((shares,)),
+            pltpu.SemaphoreType.DMA((shares,)),
+        ],
+        compiler_params=pltpu.CompilerParams(collective_id=0, has_side_effects=True),
+    )(first, second, cot)
+
+
+def products(count, out_ref, a_ref, b_ref, a_swapped, b_swapped):
+    block = 8
+    for start in range(0, count, block):
+        sums = [None] * block
+        for r in range(count):
+            if b_swapped:
+                b = b_ref[pl.ds(r, count, stride=count), :]
+            else:
+                b = b_ref[r * count : (r + 1) * count, :]
+            for place in range(block):
+                p = start + place
+                row = r * count + p if a_swapped else p * count + r
+                term = a_ref[row : row + 1, :] * b
+                sums[place] = term if sums[place] is None else sums[place] + term
+        for place in range(block):
+            p = start + place
+            out_ref[p * count : (p + 1) * count, :] = sums[place]
+
+
+def crop_layer(
+    layer,
+    incoming,
+    count,
+    pair,
+    cot,
+    gain_ref,
+    proj_ref,
+    gate_ref,
+    out_gain_ref,
+    out_w_ref,
+    left_ref,
+    right_ref,
+    cube_ref,
+    d_left_ref,
+    d_right_ref,
+):
+    gain = gain_ref[layer : layer + 1, :]
+    out_gain = out_gain_ref[layer : layer + 1, :]
+    w_proj = proj_ref[layer]
+    w_out = out_w_ref[layer]
+    width = w_out.shape[0]
+    pair_hat, pair_scale = normalize(pair, 1)
+    normed = (pair_hat * gain).astype(jnp.bfloat16)
+    projected = jnp.dot(normed, w_proj, preferred_element_type=jnp.float32)
+    a_proj = projected[:, :width]
+    b_proj = projected[:, 2 * width : 3 * width]
+    sig_a = jax.nn.sigmoid(projected[:, width : 2 * width])
+    sig_b = jax.nn.sigmoid(projected[:, 3 * width :])
+    gate = jax.nn.sigmoid(jnp.dot(normed, gate_ref[layer], preferred_element_type=jnp.float32))
+    left_ref[...] = (sig_a * a_proj).astype(jnp.bfloat16).astype(jnp.float32)
+    right_ref[...] = (sig_b * b_proj).astype(jnp.bfloat16).astype(jnp.float32)
+    if incoming:
+        products(count, cube_ref, left_ref, right_ref, True, False)
+    else:
+        products(count, cube_ref, left_ref, right_ref, False, True)
+    tri_hat, tri_scale = normalize(cube_ref[...], 1)
+    tri_norm = (tri_hat * out_gain).astype(jnp.bfloat16)
+    linear = jnp.dot(tri_norm, w_out, preferred_element_type=jnp.float32)
+    scaled = cot * gate
+    d_linear = scaled.astype(jnp.bfloat16)
+    d_gate = (cot * linear * gate * (1.0 - gate)).astype(jnp.bfloat16)
+    h = nt_dot(d_linear, w_out) * out_gain
+    cube_ref[...] = (
+        norm_back(h, tri_hat, tri_scale, 1).astype(jnp.bfloat16).astype(jnp.float32)
+    )
+    if incoming:
+        products(count, d_left_ref, right_ref, cube_ref, False, True)
+        products(count, d_right_ref, left_ref, cube_ref, False, False)
+    else:
+        products(count, d_left_ref, cube_ref, right_ref, False, False)
+        products(count, d_right_ref, cube_ref, left_ref, True, False)
+    d_left = d_left_ref[...]
+    d_right = d_right_ref[...]
+    d_proj = jnp.concatenate(
+        [
+            (d_left * sig_a).astype(jnp.bfloat16),
+            (d_left * a_proj * sig_a * (1.0 - sig_a)).astype(jnp.bfloat16),
+            (d_right * sig_b).astype(jnp.bfloat16),
+            (d_right * b_proj * sig_b * (1.0 - sig_b)).astype(jnp.bfloat16),
+        ],
+        axis=1,
+    )
+    grads = (
+        tn_dot(normed, d_proj) / count,
+        tn_dot(normed, d_gate) / count,
+        tn_dot(tri_norm, d_linear) / count,
+    )
+    return (d_proj, d_gate, grads)
+
+
+def pair_back(cot, pair, d_proj, d_gate, gain, w_proj, w_gate):
+    pair_hat, pair_scale = normalize(pair, 1)
+    d_normed = nt_dot(d_proj, w_proj) + nt_dot(d_gate, w_gate)
+    return cot + norm_back(d_normed * gain, pair_hat, pair_scale, 1)
+
+
+def crop_kernel(
+    held,
+    gain_ref,
+    proj_ref,
+    gate_ref,
+    out_gain_ref,
+    out_w_ref,
+    grad_in_ref,
+    g_proj_ref,
+    g_gate_ref,
+    g_out_ref,
+    left_ref,
+    right_ref,
+    cube_ref,
+    d_left_ref,
+    d_right_ref,
+    carried_ref,
+    d_proj_ref,
+    d_gate_ref,
+):
+    rows, count, channels = held.shape[2:]
+    scratch = (left_ref, right_ref, cube_ref, d_left_ref, d_right_ref)
+    weights = (gain_ref, proj_ref, gate_ref, out_gain_ref, out_w_ref)
+    second = held[:, 0].reshape(-1, channels).astype(jnp.float32)
+    cot = held[:, 1].reshape(-1, channels).astype(jnp.float32)
+    d_proj, d_gate, grads = crop_layer(1, True, count, second, cot, *weights, *scratch)
+    g_proj_ref[1], g_gate_ref[1], g_out_ref[1] = grads
+    carried = pair_back(
+        cot, second, d_proj, d_gate, gain_ref[1:2, :], proj_ref[1], gate_ref[1]
+    ).astype(jnp.bfloat16)
+    carried_ref[...] = carried
+    first = held[:, 2].reshape(-1, channels).astype(jnp.float32)
+    d_proj, d_gate, grads = crop_layer(
+        0, False, count, first, carried.astype(jnp.float32), *weights, *scratch
+    )
+    g_proj_ref[0], g_gate_ref[0], g_out_ref[0] = grads
+    d_proj_ref[...] = d_proj
+    d_gate_ref[...] = d_gate
+    me = lax.axis_index("ax")
+    cells = rows * count
+    mine = pl.ds(pl.multiple_of(me * cells, cells), cells)
+    d_pair = pair_back(
+        carried_ref[mine, :].astype(jnp.float32),
+        held[me, 2].reshape(cells, channels).astype(jnp.float32),
+        d_proj_ref[mine, :],
+        d_gate_ref[mine, :],
+        gain_ref[0:1, :],
+        proj_ref[0],
+        gate_ref[0],
+    )
+    grad_in_ref[...] = d_pair.astype(jnp.bfloat16).reshape(grad_in_ref.shape)
+
+
+def whole_crop(
+    pair_first, pair_second, grad_out, norm_gain, proj_weight, gate_weight, out_gain, out_weight
+):
+    shares = lax.axis_size("ax")
+    rows, count, channels = pair_first.shape
+    held = gather_rows(pair_first, pair_second, grad_out, shares)
+    cells = count * count
+    width = out_weight.shape[1]
+    vmem = pl.BlockSpec(memory_space=pltpu.VMEM)
+    f32 = jnp.float32
+    return tuple(
+        pl.pallas_call(
+            crop_kernel,
+            out_shape=(
+                jax.ShapeDtypeStruct(pair_first.shape, pair_first.dtype),
+                jax.ShapeDtypeStruct(proj_weight.shape, f32),
+                jax.ShapeDtypeStruct(gate_weight.shape, f32),
+                jax.ShapeDtypeStruct(out_weight.shape, f32),
+            ),
+            in_specs=[vmem] * 6,
+            out_specs=(vmem,) * 4,
+            scratch_shapes=[
+                pltpu.VMEM((cells, width), f32),
+                pltpu.VMEM((cells, width), f32),
+                pltpu.VMEM((cells, width), f32),
+                pltpu.VMEM((cells, width), f32),
+                pltpu.VMEM((cells, width), f32),
+                pltpu.VMEM((cells, channels), jnp.bfloat16),
+                pltpu.VMEM((cells, 4 * width), jnp.bfloat16),
+                pltpu.VMEM((cells, channels), jnp.bfloat16),
+            ],
+            compiler_params=pltpu.CompilerParams(vmem_limit_bytes=32 * 1024 * 1024),
+        )(held, norm_gain, proj_weight, gate_weight, out_gain, out_weight)
+    )
+
+
+def on_device(*args):
+    count = args[0].shape[1]
+    if count % 16 == 0 and count <= 32:
+        return whole_crop(*args)
+    return split_crop(*args)
+
+
 def solution(mesh):
     placed = (
         P(("grp", "ax"), None, None),

time: 327 us -> 17.5 us (0.05)
  blocking collectives: 152 us -> 0 us
  waiting for transfers between devices: 99.4 us -> 0 us
  starting transfers between devices: 30.3 us -> 0 us
  Pallas kernels: 0 us -> 14.7 us
  local copies, waits for them, and re-layouts: 16.3 us -> 1.89 us
  between operations: 14.5 us -> 0.71 us
  other arithmetic: 7.43 us -> 0 us
  matrix products: 5.5 us -> 0 us
    all_gather x5 -> x0, blocking collectives: 126 us -> none  [the longest x1 32.3 us: outgoing(): lax.all_gather(right_half, 'ax', axis=1, tiled=True)]
    psum x1 -> x0, waiting for transfers between devices: 88 us -> none  [on_device(): lax.psum((jnp.stack([first[1], second[1]]), jnp.stack([first[2], second[2...]
    all_to_all x8 -> x0, starting transfers between devices: 30.3 us -> none  [the longest x2 6.44 us: front(): lax.all_to_all(left_side, 'ch', split_axis=0, concat_axis=2, tiled=True)]
    all_to_all x7 -> x0, blocking collectives: 26 us -> none  [the longest x2 7.38 us: front_back(): lax.all_to_all(right_half_grad.astype(jnp.bfloat16), 'ch', split_axis=2,...]
    pallas_call x0 -> x2, Pallas kernels: none -> 14.7 us  [the longest x1 11.3 us: gather_rows(): pl.pallas_call(functools.partial(gather_kernel, shares), out_shape=jax.Sh...]
    all_to_all x8 -> x0, waiting for transfers between devices: 11.3 us -> none  [the longest x1 6.01 us: incoming(): lax.all_to_all(d_turned.astype(jnp.bfloat16), 'ax', split_axis=1, concat_...]
    unnamed x51 -> x12, local copies, waits for them, and re-layouts: 11.7 us -> 1.89 us
    dot_general x24 -> x0, matrix products: 5.5 us -> none  [the longest x2 1.16 us: front(): projected = jnp.dot(flat_normed, w_proj, preferred_element_type=jnp.float32)]
  transfers between devices with their start and end apart: 9 -> 0, of which waited for: 5 -> 0; matrix products, arithmetic and copies ran while one was open for 2% -> 0% of each run, Pallas kernels for 0% -> 0%
where the time goes in v1:
time: 17.5 us; the launch traced here: 17.3 us
  Pallas kernels  14.7 us (84%)
  local copies, waits for them, and re-layouts  1.89 us (11%)
  between operations  0.71 us (4%)
    pallas_call x1, Pallas kernels, gather_rows(): pl.pallas_call(functools.partial(gather_kernel, shares), out_shape=jax.Sh...  11.3 us
    pallas_call x1, Pallas kernels, whole_crop(): pl.pallas_call(crop_kernel, out_shape=(jax.ShapeDtypeStruct(pair_first.sh...  3.41 us
    unnamed x12, local copies, waits for them, and re-layouts  1.89 us

profile of v1, /device:TPU:0, one launch (start us, length us, event | category | flops | bytes accessed | tf_op | source)
XLA Modules:
  0.0 17.3 jit_solution(8470518625808277499)
XLA Ops:
  0.6 0.0 copy-start.3
  0.6 0.0 copy-start.5
  0.7 0.0 copy-start.2
  0.7 0.0 copy-start.4
  0.7 11.3 %shard_map.111.held = bf16[8,3,2,16,128]{4,3,2,1,0:T(8,128)(2,1)} custom-call(bf16[2,16,128]{2,1,0:T(8,128)(2,1)} %first_ref.1, bf16[2,16,128]{2,1,0:T(8,128)(2,1)} %second_ref.1, bf16[2,16,128]{2,1,0:T(8,128)(2,1)} %cot_ref.1), custom_call_target="tpu_custom_call" | custom-call | tf_op jit(solution)/shard_map/pallas_call | solution.py:287
  12.0 0.0 copy-done.3
  12.0 0.0 copy-done.5
  12.0 0.0 copy-done.2
  12.0 0.0 copy-done.4
  12.0 0.0 copy-start
  12.0 0.9 %copy-done = bf16[8,3,2,16,128]{4,3,2,1,0:T(8,128)(2,1)S(1)} copy-done((bf16[8,3,2,16,128]{4,3,2,1,0:T(8,128)(2,1)S(1)}, bf16[8,3,2,16,128]{4,3,2,1,0:T(8,128)(2,1)}, u32[]{:S(2)}) %copy-start) | copy-done | bytes 196632
  12.9 0.0 copy-start.1
  12.9 0.9 %copy-done.1 = bf16[2,128,512]{2,1,0:T(8,128)(2,1)S(1)} copy-done((bf16[2,128,512]{2,1,0:T(8,128)(2,1)S(1)}, bf16[2,128,512]{2,1,0:T(8,128)(2,1)}, u32[]{:S(2)}) %copy-start.1) | copy-done | bytes 262168
  13.9 3.4 %shard_map.112 = (bf16[2,16,128]{2,1,0:T(8,128)(2,1)}, f32[2,128,512]{2,1,0:T(8,128)}, f32[2,128,128]{2,1,0:T(8,128)}, f32[2,128,128]{2,1,0:T(8,128)}) custom-call(bf16[8,3,2,16,128]{4,3,2,1,0:T(8,128)(2,1)S(1)} %copy-done, f32[2,128]{1,0:T(2,128)S(1)} %copy-done.4, bf16[2,128,512]{2,1,0:T(8,128)(2,1)S(1)} %copy-done.1, bf16[2,128,128]{2,1,0:T(8,128)(2,1)S(1)} %copy-done.2, ...), custom_call_target="tpu_custom_call" | custom-call | tf_op jit(solution)/shard_map/pallas_call | solution.py:460
Async XLA Ops:
  0.6 11.3 %copy-start.3 = (bf16[2,128,128]{2,1,0:T(8,128)(2,1)S(1)}, bf16[2,128,128]{2,1,0:T(8,128)(2,1)}, u32[]{:S(2)}) copy-start(bf16[2,128,128]{2,1,0:T(8,128)(2,1)} %out_w_ref.1) | copy-start | bytes 196612
  0.6 11.3 %copy-start.5 = (f32[2,128]{1,0:T(2,128)S(1)}, f32[2,128]{1,0:T(2,128)}, u32[]{:S(2)}) copy-start(f32[2,128]{1,0:T(2,128)} %out_gain_ref.1) | copy-start | bytes 3076
  0.7 11.3 %copy-start.2 = (bf16[2,128,128]{2,1,0:T(8,128)(2,1)S(1)}, bf16[2,128,128]{2,1,0:T(8,128)(2,1)}, u32[]{:S(2)}) copy-start(bf16[2,128,128]{2,1,0:T(8,128)(2,1)} %gate_ref.1) | copy-start | bytes 196612
  0.7 11.3 %copy-start.4 = (f32[2,128]{1,0:T(2,128)S(1)}, f32[2,128]{1,0:T(2,128)}, u32[]{:S(2)}) copy-start(f32[2,128]{1,0:T(2,128)} %gain_ref.1) | copy-start | bytes 3076
  12.0 0.9 %copy-start = (bf16[8,3,2,16,128]{4,3,2,1,0:T(8,128)(2,1)S(1)}, bf16[8,3,2,16,128]{4,3,2,1,0:T(8,128)(2,1)}, u32[]{:S(2)}) copy-start(bf16[8,3,2,16,128]{4,3,2,1,0:T(8,128)(2,1)} %shard_map.111.held) | copy-start | bytes 589828
  12.9 0.9 %copy-start.1 = (bf16[2,128,512]{2,1,0:T(8,128)(2,1)S(1)}, bf16[2,128,512]{2,1,0:T(8,128)(2,1)}, u32[]{:S(2)}) copy-start(bf16[2,128,512]{2,1,0:T(8,128)(2,1)} %proj_ref.1) | copy-start | bytes 786436

commit v2 on v1

--- a/solution.py
+++ b/solution.py
@@ -254,47 +254,103 @@
     return lax.dot_general(a, b, (((0,), (0,)), ((), ())), preferred_element_type=jnp.float32)
 
 
-def gather_kernel(shares, first_ref, second_ref, cot_ref, held, send_sem, recv_sem):
+def gather_kernel(shares, halves, first_ref, second_ref, cot_ref, *rest):
+    weight_refs, held, weight_outs = rest[:5], rest[5], rest[6:11]
+    stage_sem, weight_sem, send_sem, recv_sem, pass_sem, got_sem = rest[11:]
     me = lax.axis_index("ax")
+    core = lax.axis_index("ch")
+    part = held.shape[3]
+    mesh_id = pl.DeviceIdType.MESH
+    near_first = sorted(range(1, shares), key=lambda step: min(step, shares - step))
     barrier = pltpu.get_barrier_semaphore()
-    for step in range(1, shares):
+    for step in reversed(near_first):
         peer = lax.rem(me + step, shares)
-        pl.semaphore_signal(
-            barrier, inc=1, device_id={"ax": peer}, device_id_type=pl.DeviceIdType.MESH
-        )
-    held[me, 0] = second_ref[...]
-    held[me, 1] = cot_ref[...]
-    held[me, 2] = first_ref[...]
-    pl.semaphore_wait(barrier, shares - 1)
-    copies = []
-    for step in range(1, shares):
+        pl.semaphore_signal(barrier, inc=1, device_id={"ax": peer}, device_id_type=mesh_id)
+    for turn in range(1, halves):
+        mate = lax.rem(core + turn, halves)
+        pl.semaphore_signal(barrier, inc=1, device_id={"ch": mate}, device_id_type=mesh_id)
+    staged = []
+    for place, ref in enumerate((second_ref, cot_ref, first_ref)):
+        for half in range(halves):
+            copy = pltpu.make_async_copy(
+                ref.at[pl.ds(half * part, part)],
+                held.at[me, half, place],
+                stage_sem.at[place, half],
+            )
+            copy.start()
+            staged.append(copy)
+    loads = [
+        pltpu.make_async_copy(ref, out, weight_sem.at[place])
+        for place, (ref, out) in enumerate(zip(weight_refs, weight_outs))
+    ]
+    for copy in loads:
+        copy.start()
+    for copy in staged:
+        copy.wait()
+    pl.semaphore_wait(barrier, shares + halves - 2)
+    sends = {}
+    for step in reversed(near_first):
         peer = lax.rem(me + step, shares)
-        copy = pltpu.make_async_remote_copy(
-            src_ref=held.at[me],
-            dst_ref=held.at[me],
+        sends[step] = pltpu.make_async_remote_copy(
+            src_ref=held.at[me, core],
+            dst_ref=held.at[me, core],
             send_sem=send_sem.at[step],
             recv_sem=recv_sem.at[step],
             device_id={"ax": peer},
-            device_id_type=pl.DeviceIdType.MESH,
+            device_id_type=mesh_id,
         )
-        copy.start()
-        copies.append(copy)
-    for copy in copies:
+        sends[step].start()
+    passes = []
+    for step in near_first:
+        source = lax.rem(me - step + shares, shares)
+        sends[step].wait_recv()
+        for turn in range(1, halves):
+            mate = lax.rem(core + turn, halves)
+            copy = pltpu.make_async_remote_copy(
+                src_ref=held.at[source, core],
+                dst_ref=held.at[source, core],
+                send_sem=pass_sem.at[step, turn],
+                recv_sem=got_sem.at[step, turn],
+                device_id={"ch": mate},
+                device_id_type=mesh_id,
+            )
+            copy.start()
+            passes.append(copy)
+    for copy in passes:
+        copy.wait_recv()
+    for step in near_first:
+        sends[step].wait_send()
+    for copy in passes:
+        copy.wait_send()
+    for copy in loads:
         copy.wait()
 
 
-def gather_rows(first, second, cot, shares):
+def gather_rows(first, second, cot, weights, shares, halves):
+    rows, count, channels = first.shape
+    shape = (shares, halves, 3, rows // halves, count, channels)
+    hbm = pl.BlockSpec(memory_space=pltpu.HBM)
+    vmem = pl.BlockSpec(memory_space=pltpu.VMEM)
     return pl.pallas_call(
-        functools.partial(gather_kernel, shares),
-        out_shape=jax.ShapeDtypeStruct((shares, 3) + first.shape, first.dtype),
-        in_specs=[pl.BlockSpec(memory_space=pltpu.VMEM)] * 3,
-        out_specs=pl.BlockSpec(memory_space=pltpu.VMEM),
+        functools.partial(gather_kernel, shares, halves),
+        out_shape=(
+            pltpu.VMEM(shape, first.dtype),
+            *(pltpu.VMEM(weight.shape, weight.dtype) for weight in weights),
+        ),
+        in_specs=[hbm] * 8,
+        out_specs=(vmem,) * 6,
         scratch_shapes=[
+            pltpu.SemaphoreType.DMA((3, halves)),
+            pltpu.SemaphoreType.DMA((5,)),
             pltpu.SemaphoreType.DMA((shares,)),
             pltpu.SemaphoreType.DMA((shares,)),
+            pltpu.SemaphoreType.DMA((shares, halves)),
+            pltpu.SemaphoreType.DMA((shares, halves)),
         ],
-        compiler_params=pltpu.CompilerParams(collective_id=0, has_side_effects=True),
-    )(first, second, cot)
+        compiler_params=pltpu.CompilerParams(
+            collective_id=0, has_side_effects=True, vmem_limit_bytes=4 * 1024 * 1024
+        ),
+    )(*(pltpu.with_memory_space_constraint(x, pltpu.HBM) for x in (first, second, cot, *weights)))
 
 
 def products(count, out_ref, a_ref, b_ref, a_swapped, b_swapped):
@@ -413,18 +469,19 @@
     d_proj_ref,
     d_gate_ref,
 ):
-    rows, count, channels = held.shape[2:]
+    count, channels = held.shape[4:]
+    rows = held.shape[1] * held.shape[3]
     scratch = (left_ref, right_ref, cube_ref, d_left_ref, d_right_ref)
     weights = (gain_ref, proj_ref, gate_ref, out_gain_ref, out_w_ref)
-    second = held[:, 0].reshape(-1, channels).astype(jnp.float32)
-    cot = held[:, 1].reshape(-1, channels).astype(jnp.float32)
+    second = held[:, :, 0].reshape(-1, channels).astype(jnp.float32)
+    cot = held[:, :, 1].reshape(-1, channels).astype(jnp.float32)
     d_proj, d_gate, grads = crop_layer(1, True, count, second, cot, *weights, *scratch)
     g_proj_ref[1], g_gate_ref[1], g_out_ref[1] = grads
     carried = pair_back(
         cot, second, d_proj, d_gate, gain_ref[1:2, :], proj_ref[1], gate_ref[1]
     ).astype(jnp.bfloat16)
     carried_ref[...] = carried
-    first = held[:, 2].reshape(-1, channels).astype(jnp.float32)
+    first = held[:, :, 2].reshape(-1, channels).astype(jnp.float32)
     d_proj, d_gate, grads = crop_layer(
         0, False, count, first, carried.astype(jnp.float32), *weights, *scratch
     )
@@ -436,7 +493,7 @@
     mine = pl.ds(pl.multiple_of(me * cells, cells), cells)
     d_pair = pair_back(
         carried_ref[mine, :].astype(jnp.float32),
-        held[me, 2].reshape(cells, channels).astype(jnp.float32),
+        held[me, :, 2].reshape(cells, channels).astype(jnp.float32),
         d_proj_ref[mine, :],
         d_gate_ref[mine, :],
         gain_ref[0:1, :],
@@ -451,7 +508,10 @@
 ):
     shares = lax.axis_size("ax")
     rows, count, channels = pair_first.shape
-    held = gather_rows(pair_first, pair_second, grad_out, shares)
+    weights = (norm_gain, proj_weight, gate_weight, out_gain, out_weight)
+    placed = gather_rows(
+        pair_first, pair_second, grad_out, weights, shares, lax.axis_size("ch")
+    )
     cells = count * count
     width = out_weight.shape[1]
     vmem = pl.BlockSpec(memory_space=pltpu.VMEM)
@@ -477,14 +537,14 @@
                 pltpu.VMEM((cells, 4 * width), jnp.bfloat16),
                 pltpu.VMEM((cells, channels), jnp.bfloat16),
             ],
-            compiler_params=pltpu.CompilerParams(vmem_limit_bytes=32 * 1024 * 1024),
-        )(held, norm_gain, proj_weight, gate_weight, out_gain, out_weight)
+            compiler_params=pltpu.CompilerParams(vmem_limit_bytes=16 * 1024 * 1024),
+        )(*placed)
     )
 
 
 def on_device(*args):
-    count = args[0].shape[1]
-    if count % 16 == 0 and count <= 32:
+    rows, count = args[0].shape[:2]
+    if count % 16 == 0 and count <= 32 and rows % lax.axis_size("ch") == 0:
         return whole_crop(*args)
     return split_crop(*args)
 

time: 17.5 us -> 15 us (0.86)
  local copies, waits for them, and re-layouts: 1.89 us -> 0 us
  Pallas kernels: 14.7 us -> 14.2 us
    unnamed x12 -> x0, local copies, waits for them, and re-layouts: 1.89 us -> none
    pallas_call x1, Pallas kernels: 11.3 us -> 10.8 us  [gather_rows(): pl.pallas_call(functools.partial(gather_kernel, shares, halves), out_shap...]
where the time goes in v2:
time: 15 us; the launch traced here: 14.8 us
  Pallas kernels  14.2 us (95%)
  between operations  0.64 us (4%)
    pallas_call x1, Pallas kernels, gather_rows(): pl.pallas_call(functools.partial(gather_kernel, shares, halves), out_shap...  10.8 us
    pallas_call x1, Pallas kernels, whole_crop(): pl.pallas_call(crop_kernel, out_shape=(jax.ShapeDtypeStruct(pair_first.sh...  3.41 us

profile of v2, /device:TPU:0, one launch (start us, length us, event | category | flops | bytes accessed | tf_op | source)
XLA Modules:
  0.0 14.8 jit_solution(17947700965090163533)
XLA Ops:
  0.6 10.8 %shard_map.111 = (bf16[8,2,3,1,16,128]{5,4,3,2,1,0:T(8,128)(2,1)S(1)}, f32[2,128]{1,0:T(2,128)S(1)}, bf16[2,128,512]{2,1,0:T(8,128)(2,1)S(1)}, bf16[2,128,128]{2...) custom-call(bf16[2,16,128]{2,1,0:T(8,128)(2,1)} %first_ref.1, ...), custom_call_target="tpu_custom_call" | custom-call | tf_op jit(solution)/shard_map/pallas_call | solution.py:334
  11.4 3.4 %shard_map.112 = (bf16[2,16,128]{2,1,0:T(8,128)(2,1)}, f32[2,128,512]{2,1,0:T(8,128)}, f32[2,128,128]{2,1,0:T(8,128)}, f32[2,128,128]{2,1,0:T(8,128)}) custom-call(bf16[8,2,3,1,16,128]{5,4,3,2,1,0:T(8,128)(2,1)S(1)} %get-tuple-element.10.held, f32[2,128]{1,0:T(2,128)S(1)} %get-tuple-element.11.gain_ref, bf16[2,128,512]{2,1,0:T(8,128)(2,1)S(1)} %get-tuple-element.12.proj_ref, ...), custom_call_target="tpu_custom_call" | custom-call | tf_op jit(solution)/shard_map/pallas_call | solution.py:520

commit v3 on v1

--- a/solution.py
+++ b/solution.py
@@ -254,49 +254,6 @@
     return lax.dot_general(a, b, (((0,), (0,)), ((), ())), preferred_element_type=jnp.float32)
 
 
-def gather_kernel(shares, first_ref, second_ref, cot_ref, held, send_sem, recv_sem):
-    me = lax.axis_index("ax")
-    barrier = pltpu.get_barrier_semaphore()
-    for step in range(1, shares):
-        peer = lax.rem(me + step, shares)
-        pl.semaphore_signal(
-            barrier, inc=1, device_id={"ax": peer}, device_id_type=pl.DeviceIdType.MESH
-        )
-    held[me, 0] = second_ref[...]
-    held[me, 1] = cot_ref[...]
-    held[me, 2] = first_ref[...]
-    pl.semaphore_wait(barrier, shares - 1)
-    copies = []
-    for step in range(1, shares):
-        peer = lax.rem(me + step, shares)
-        copy = pltpu.make_async_remote_copy(
-            src_ref=held.at[me],
-            dst_ref=held.at[me],
-            send_sem=send_sem.at[step],
-            recv_sem=recv_sem.at[step],
-            device_id={"ax": peer},
-            device_id_type=pl.DeviceIdType.MESH,
-        )
-        copy.start()
-        copies.append(copy)
-    for copy in copies:
-        copy.wait()
-
-
-def gather_rows(first, second, cot, shares):
-    return pl.pallas_call(
-        functools.partial(gather_kernel, shares),
-        out_shape=jax.ShapeDtypeStruct((shares, 3) + first.shape, first.dtype),
-        in_specs=[pl.BlockSpec(memory_space=pltpu.VMEM)] * 3,
-        out_specs=pl.BlockSpec(memory_space=pltpu.VMEM),
-        scratch_shapes=[
-            pltpu.SemaphoreType.DMA((shares,)),
-            pltpu.SemaphoreType.DMA((shares,)),
-        ],
-        compiler_params=pltpu.CompilerParams(collective_id=0, has_side_effects=True),
-    )(first, second, cot)
-
-
 def products(count, out_ref, a_ref, b_ref, a_swapped, b_swapped):
     block = 8
     for start in range(0, count, block):
@@ -321,7 +278,7 @@
     incoming,
     count,
     pair,
-    cot,
+    fetch_cot,
     gain_ref,
     proj_ref,
     gate_ref,
@@ -355,6 +312,7 @@
     tri_hat, tri_scale = normalize(cube_ref[...], 1)
     tri_norm = (tri_hat * out_gain).astype(jnp.bfloat16)
     linear = jnp.dot(tri_norm, w_out, preferred_element_type=jnp.float32)
+    cot = fetch_cot()
     scaled = cot * gate
     d_linear = scaled.astype(jnp.bfloat16)
     d_gate = (cot * linear * gate * (1.0 - gate)).astype(jnp.bfloat16)
@@ -384,7 +342,7 @@
         tn_dot(normed, d_gate) / count,
         tn_dot(tri_norm, d_linear) / count,
     )
-    return (d_proj, d_gate, grads)
+    return (d_proj, d_gate, grads, cot)
 
 
 def pair_back(cot, pair, d_proj, d_gate, gain, w_proj, w_gate):
@@ -393,42 +351,97 @@
     return cot + norm_back(d_normed * gain, pair_hat, pair_scale, 1)
 
 
-def crop_kernel(
-    held,
-    gain_ref,
-    proj_ref,
-    gate_ref,
-    out_gain_ref,
-    out_w_ref,
-    grad_in_ref,
-    g_proj_ref,
-    g_gate_ref,
-    g_out_ref,
-    left_ref,
-    right_ref,
-    cube_ref,
-    d_left_ref,
-    d_right_ref,
-    carried_ref,
-    d_proj_ref,
-    d_gate_ref,
-):
+def second_kernel(shares, first_ref, second_ref, cot_ref, *rest):
+    weight_refs, held, carried_ref, g_refs, weights = (
+        rest[:5],
+        rest[5],
+        rest[6],
+        rest[7:10],
+        rest[10:15],
+    )
+    scratch, (stage_sem, weight_sem, send_sem, recv_sem) = rest[15:20], rest[20:]
+    me = lax.axis_index("ax")
+    count, channels = held.shape[3:]
+    mesh_id = pl.DeviceIdType.MESH
+    near_first = sorted(range(1, shares), key=lambda step: min(step, shares - step))
+    barrier = pltpu.get_barrier_semaphore()
+    for step in reversed(near_first):
+        peer = lax.rem(me + step, shares)
+        pl.semaphore_signal(barrier, inc=1, device_id={"ax": peer}, device_id_type=mesh_id)
+    staged = []
+    for place, ref in enumerate((second_ref, cot_ref, first_ref)):
+        staged.append(pltpu.make_async_copy(ref, held.at[me, place], stage_sem.at[place]))
+    loads = [
+        pltpu.make_async_copy(ref, out, weight_sem.at[place])
+        for place, (ref, out) in enumerate(zip(weight_refs, weights))
+    ]
+    for copy in staged + loads:
+        copy.start()
+    for copy in staged:
+        copy.wait()
+    pl.semaphore_wait(barrier, shares - 1)
+    sends = []
+    for place in range(3):
+        group = []
+        for step in reversed(near_first):
+            peer = lax.rem(me + step, shares)
+            copy = pltpu.make_async_remote_copy(
+                src_ref=held.at[me, place],
+                dst_ref=held.at[me, place],
+                send_sem=send_sem.at[place, step],
+                recv_sem=recv_sem.at[place, step],
+                device_id={"ax": peer},
+                device_id_type=mesh_id,
+            )
+            copy.start()
+            group.append(copy)
+        sends.append(group)
+    for copy in loads:
+        copy.wait()
+
+    def arrived(place):
+        for copy in sends[place]:
+            copy.wait_recv()
+        return held[:, place].reshape(-1, channels).astype(jnp.float32)
+
+    second = arrived(0)
+    d_proj, d_gate, grads, cot = crop_layer(
+        1, True, count, second, lambda: arrived(1), *weights, *scratch
+    )
+    for ref, grad in zip(g_refs, grads):
+        ref[...] = grad
+    carried_ref[...] = pair_back(
+        cot, second, d_proj, d_gate, weights[0][1:2, :], weights[1][1], weights[2][1]
+    ).astype(jnp.bfloat16)
+    for copy in sends[2]:
+        copy.wait_recv()
+    for group in sends:
+        for copy in group:
+            copy.wait_send()
+
+
+def first_kernel(held, carried_ref, *rest):
+    g_seconds, weights = rest[:3], rest[3:8]
+    grad_in_ref, g_outs = rest[8], rest[9:12]
+    g_firsts, scratch = rest[12:15], rest[15:20]
+    d_proj_ref, d_gate_ref, first_sem, second_sem = rest[20:]
     rows, count, channels = held.shape[2:]
-    scratch = (left_ref, right_ref, cube_ref, d_left_ref, d_right_ref)
-    weights = (gain_ref, proj_ref, gate_ref, out_gain_ref, out_w_ref)
-    second = held[:, 0].reshape(-1, channels).astype(jnp.float32)
-    cot = held[:, 1].reshape(-1, channels).astype(jnp.float32)
-    d_proj, d_gate, grads = crop_layer(1, True, count, second, cot, *weights, *scratch)
-    g_proj_ref[1], g_gate_ref[1], g_out_ref[1] = grads
-    carried = pair_back(
-        cot, second, d_proj, d_gate, gain_ref[1:2, :], proj_ref[1], gate_ref[1]
-    ).astype(jnp.bfloat16)
-    carried_ref[...] = carried
+    copies = []
+    for place in range(3):
+        copies.append(
+            pltpu.make_async_copy(g_seconds[place], g_outs[place].at[1], second_sem.at[place])
+        )
+        copies[-1].start()
     first = held[:, 2].reshape(-1, channels).astype(jnp.float32)
-    d_proj, d_gate, grads = crop_layer(
-        0, False, count, first, carried.astype(jnp.float32), *weights, *scratch
-    )
-    g_proj_ref[0], g_gate_ref[0], g_out_ref[0] = grads
+    d_proj, d_gate, grads, _ = crop_layer(
+        0, False, count, first, lambda: carried_ref[...].astype(jnp.float32), *weights, *scratch
+    )
+    for place in range(3):
+        g_firsts[place][...] = grads[place]
+        copies.append(
+            pltpu.make_async_copy(g_firsts[place], g_outs[place].at[0], first_sem.at[place])
+        )
+        copies[-1].start()
     d_proj_ref[...] = d_proj
     d_gate_ref[...] = d_gate
     me = lax.axis_index("ax")
@@ -439,11 +452,13 @@
         held[me, 2].reshape(cells, channels).astype(jnp.float32),
         d_proj_ref[mine, :],
         d_gate_ref[mine, :],
-        gain_ref[0:1, :],
-        proj_ref[0],
-        gate_ref[0],
+        weights[0][0:1, :],
+        weights[1][0],
+        weights[2][0],
     )
     grad_in_ref[...] = d_pair.astype(jnp.bfloat16).reshape(grad_in_ref.shape)
+    for copy in copies:
+        copy.wait()
 
 
 def whole_crop(
@@ -451,34 +466,55 @@
 ):
     shares = lax.axis_size("ax")
     rows, count, channels = pair_first.shape
-    held = gather_rows(pair_first, pair_second, grad_out, shares)
     cells = count * count
     width = out_weight.shape[1]
+    weights = (norm_gain, proj_weight, gate_weight, out_gain, out_weight)
+    matrices = (proj_weight, gate_weight, out_weight)
     vmem = pl.BlockSpec(memory_space=pltpu.VMEM)
+    hbm = pl.BlockSpec(memory_space=pltpu.HBM)
     f32 = jnp.float32
+    cubes = [pltpu.VMEM((cells, width), f32) for _ in range(5)]
+    args = (pair_first, pair_second, grad_out) + weights
+    placed = pl.pallas_call(
+        functools.partial(second_kernel, shares),
+        out_shape=(
+            pltpu.VMEM((shares, 3) + pair_first.shape, pair_first.dtype),
+            pltpu.VMEM((cells, channels), jnp.bfloat16),
+            *(pltpu.VMEM(matrix.shape[1:], f32) for matrix in matrices),
+            *(pltpu.VMEM(weight.shape, weight.dtype) for weight in weights),
+        ),
+        in_specs=[hbm] * 8,
+        out_specs=(vmem,) * 10,
+        scratch_shapes=cubes
+        + [
+            pltpu.SemaphoreType.DMA((3,)),
+            pltpu.SemaphoreType.DMA((5,)),
+            pltpu.SemaphoreType.DMA((3, shares)),
+            pltpu.SemaphoreType.DMA((3, shares)),
+        ],
+        compiler_params=pltpu.CompilerParams(
+            collective_id=0, has_side_effects=True, vmem_limit_bytes=16 * 1024 * 1024
+        ),
+    )(*(pltpu.with_memory_space_constraint(arg, pltpu.HBM) for arg in args))
     return tuple(
         pl.pallas_call(
-            crop_kernel,
+            first_kernel,
             out_shape=(
                 jax.ShapeDtypeStruct(pair_first.shape, pair_first.dtype),
-                jax.ShapeDtypeStruct(proj_weight.shape, f32),
-                jax.ShapeDtypeStruct(gate_weight.shape, f32),
-                jax.ShapeDtypeStruct(out_weight.shape, f32),
+                *(jax.ShapeDtypeStruct(matrix.shape, f32) for matrix in matrices),
             ),
-            in_specs=[vmem] * 6,
-            out_specs=(vmem,) * 4,
-            scratch_shapes=[
-                pltpu.VMEM((cells, width), f32),
-                pltpu.VMEM((cells, width), f32),
-                pltpu.VMEM((cells, width), f32),
-                pltpu.VMEM((cells, width), f32),
-                pltpu.VMEM((cells, width), f32),
-                pltpu.VMEM((cells, channels), jnp.bfloat16),
+            in_specs=[vmem] * 10,
+            out_specs=(vmem, hbm, hbm, hbm),
+            scratch_shapes=[pltpu.VMEM(matrix.shape[1:], f32) for matrix in matrices]
+            + cubes
+            + [
                 pltpu.VMEM((cells, 4 * width), jnp.bfloat16),
                 pltpu.VMEM((cells, channels), jnp.bfloat16),
+                pltpu.SemaphoreType.DMA((3,)),
+                pltpu.SemaphoreType.DMA((3,)),
             ],
-            compiler_params=pltpu.CompilerParams(vmem_limit_bytes=32 * 1024 * 1024),
-        )(held, norm_gain, proj_weight, gate_weight, out_gain, out_weight)
+            compiler_params=pltpu.CompilerParams(vmem_limit_bytes=16 * 1024 * 1024),
+        )(*placed)
     )
 
 

time: 17.5 us -> 15.7 us (0.90)
  local copies, waits for them, and re-layouts: 1.89 us -> 0 us
  Pallas kernels: 14.7 us -> 14.9 us
    unnamed x12 -> x0, local copies, waits for them, and re-layouts: 1.89 us -> none
    pallas_call x2, Pallas kernels: 14.7 us -> 14.9 us  [the longest x1 12.2 us: whole_crop(): pl.pallas_call(functools.partial(second_kernel, shares), out_shape=(pltpu...]
where the time goes in v3:
time: 15.7 us; the launch traced here: 15.6 us
  Pallas kernels  14.9 us (95%)
  between operations  0.64 us (4%)
    pallas_call x1, Pallas kernels, whole_crop(): pl.pallas_call(functools.partial(second_kernel, shares), out_shape=(pltpu...  12.2 us
    pallas_call x1, Pallas kernels, whole_crop(): pl.pallas_call(first_kernel, out_shape=(jax.ShapeDtypeStruct(pair_first.s...  2.74 us

profile of v3, /device:TPU:0, one launch (start us, length us, event | category | flops | bytes accessed | tf_op | source)
XLA Modules:
  0.0 15.6 jit_solution(1968836102099136496)
XLA Ops:
  0.6 12.2 %shard_map.111 = (bf16[8,3,2,16,128]{4,3,2,1,0:T(8,128)(2,1)S(1)}, bf16[256,128]{1,0:T(8,128)(2,1)S(1)}, f32[128,512]{1,0:T(8,128)S(1)}, f32[128,128]{1,0:T(8,12...) custom-call(bf16[2,16,128]{2,1,0:T(8,128)(2,1)} %first_ref.1, ...), custom_call_target="tpu_custom_call" | custom-call | tf_op jit(solution)/shard_map/pallas_call | solution.py:478
  12.8 2.7 %shard_map.112 = (bf16[2,16,128]{2,1,0:T(8,128)(2,1)}, f32[2,128,512]{2,1,0:T(8,128)}, f32[2,128,128]{2,1,0:T(8,128)}, f32[2,128,128]{2,1,0:T(8,128)}) custom-call(bf16[8,3,2,16,128]{4,3,2,1,0:T(8,128)(2,1)S(1)} %get-tuple-element.14.held, bf16[256,128]{1,0:T(8,128)(2,1)S(1)} %get-tuple-element.15.carried_ref, f32[128,512]{1,0:T(8,128)S(1)} %get-tuple-element.16.rest_0_, ...), custom_call_target="tpu_custom_call" | custom-call | tf_op jit(solution)/shard_map/pallas_call | solution.py:500

commit v4 on v2

--- a/solution.py
+++ b/solution.py
@@ -283,8 +283,6 @@
         pltpu.make_async_copy(ref, out, weight_sem.at[place])
         for place, (ref, out) in enumerate(zip(weight_refs, weight_outs))
     ]
-    for copy in loads:
-        copy.start()
     for copy in staged:
         copy.wait()
     pl.semaphore_wait(barrier, shares + halves - 2)
@@ -300,6 +298,8 @@
             device_id_type=mesh_id,
         )
         sends[step].start()
+    for copy in loads:
+        copy.start()
     passes = []
     for step in near_first:
         source = lax.rem(me - step + shares, shares)
@@ -468,6 +468,10 @@
     carried_ref,
     d_proj_ref,
     d_gate_ref,
+    held_g_proj,
+    held_g_gate,
+    held_g_out,
+    write_sem,
 ):
     count, channels = held.shape[4:]
     rows = held.shape[1] * held.shape[3]
@@ -475,8 +479,22 @@
     weights = (gain_ref, proj_ref, gate_ref, out_gain_ref, out_w_ref)
     second = held[:, :, 0].reshape(-1, channels).astype(jnp.float32)
     cot = held[:, :, 1].reshape(-1, channels).astype(jnp.float32)
+    g_held = (held_g_proj, held_g_gate, held_g_out)
+    g_outs = (g_proj_ref, g_gate_ref, g_out_ref)
+    writes = []
+
+    def write_out(layer, grads):
+        for place in range(3):
+            g_held[place][layer] = grads[place]
+            writes.append(
+                pltpu.make_async_copy(
+                    g_held[place].at[layer], g_outs[place].at[layer], write_sem.at[layer, place]
+                )
+            )
+            writes[-1].start()
+
     d_proj, d_gate, grads = crop_layer(1, True, count, second, cot, *weights, *scratch)
-    g_proj_ref[1], g_gate_ref[1], g_out_ref[1] = grads
+    write_out(1, grads)
     carried = pair_back(
         cot, second, d_proj, d_gate, gain_ref[1:2, :], proj_ref[1], gate_ref[1]
     ).astype(jnp.bfloat16)
@@ -485,7 +503,7 @@
     d_proj, d_gate, grads = crop_layer(
         0, False, count, first, carried.astype(jnp.float32), *weights, *scratch
     )
-    g_proj_ref[0], g_gate_ref[0], g_out_ref[0] = grads
+    write_out(0, grads)
     d_proj_ref[...] = d_proj
     d_gate_ref[...] = d_gate
     me = lax.axis_index("ax")
@@ -501,6 +519,8 @@
         gate_ref[0],
     )
     grad_in_ref[...] = d_pair.astype(jnp.bfloat16).reshape(grad_in_ref.shape)
+    for copy in writes:
+        copy.wait()
 
 
 def whole_crop(
@@ -515,6 +535,7 @@
     cells = count * count
     width = out_weight.shape[1]
     vmem = pl.BlockSpec(memory_space=pltpu.VMEM)
+    hbm = pl.BlockSpec(memory_space=pltpu.HBM)
     f32 = jnp.float32
     return tuple(
         pl.pallas_call(
@@ -526,7 +547,7 @@
                 jax.ShapeDtypeStruct(out_weight.shape, f32),
             ),
             in_specs=[vmem] * 6,
-            out_specs=(vmem,) * 4,
+            out_specs=(vmem,) + (hbm,) * 3,
             scratch_shapes=[
                 pltpu.VMEM((cells, width), f32),
                 pltpu.VMEM((cells, width), f32),
@@ -536,6 +557,10 @@
                 pltpu.VMEM((cells, channels), jnp.bfloat16),
                 pltpu.VMEM((cells, 4 * width), jnp.bfloat16),
                 pltpu.VMEM((cells, channels), jnp.bfloat16),
+                pltpu.VMEM(proj_weight.shape, f32),
+                pltpu.VMEM(gate_weight.shape, f32),
+                pltpu.VMEM(out_weight.shape, f32),
+                pltpu.SemaphoreType.DMA((2, 3)),
             ],
             compiler_params=pltpu.CompilerParams(vmem_limit_bytes=16 * 1024 * 1024),
         )(*placed)

time: 15 us -> 15.4 us (1.027)
  Pallas kernels: 14.2 us -> 14.6 us
    pallas_call x1, Pallas kernels: 3.41 us -> 3.92 us  [whole_crop(): pl.pallas_call(crop_kernel, out_shape=(jax.ShapeDtypeStruct(pair_first.sh...]
where the time goes in v4:
time: 15.4 us; the launch traced here: 15.2 us
  Pallas kernels  14.6 us (95%)
  between operations  0.64 us (4%)
    pallas_call x1, Pallas kernels, gather_rows(): pl.pallas_call(functools.partial(gather_kernel, shares, halves), out_shap...  10.7 us
    pallas_call x1, Pallas kernels, whole_crop(): pl.pallas_call(crop_kernel, out_shape=(jax.ShapeDtypeStruct(pair_first.sh...  3.92 us

profile of v4, /device:TPU:0, one launch (start us, length us, event | category | flops | bytes accessed | tf_op | source)
XLA Modules:
  0.0 15.2 jit_solution(2164161967882933636)
XLA Ops:
  0.6 10.7 %shard_map.111 = (bf16[8,2,3,1,16,128]{5,4,3,2,1,0:T(8,128)(2,1)S(1)}, f32[2,128]{1,0:T(2,128)S(1)}, bf16[2,128,512]{2,1,0:T(8,128)(2,1)S(1)}, bf16[2,128,128]{2...) custom-call(bf16[2,16,128]{2,1,0:T(8,128)(2,1)} %first_ref.1, ...), custom_call_target="tpu_custom_call" | custom-call | tf_op jit(solution)/shard_map/pallas_call | solution.py:334
  11.3 3.9 %shard_map.112 = (bf16[2,16,128]{2,1,0:T(8,128)(2,1)}, f32[2,128,512]{2,1,0:T(8,128)}, f32[2,128,128]{2,1,0:T(8,128)}, f32[2,128,128]{2,1,0:T(8,128)}) custom-call(bf16[8,2,3,1,16,128]{5,4,3,2,1,0:T(8,128)(2,1)S(1)} %get-tuple-element.10.held, f32[2,128]{1,0:T(2,128)S(1)} %get-tuple-element.11.gain_ref, bf16[2,128,512]{2,1,0:T(8,128)(2,1)S(1)} %get-tuple-element.12.proj_ref, ...), custom_call_target="tpu_custom_call" | custom-call | tf_op jit(solution)/shard_map/pallas_call | solution.py:541

commit v5 on v2

--- a/solution.py
+++ b/solution.py
@@ -354,7 +354,7 @@
 
 
 def products(count, out_ref, a_ref, b_ref, a_swapped, b_swapped):
-    block = 8
+    block = 16
     for start in range(0, count, block):
         sums = [None] * block
         for r in range(count):

time: 15 us -> 15 us (level)
  no operation moved by 1% of the time
where the time goes in v5:
time: 15 us; the launch traced here: 14.8 us
  Pallas kernels  14.2 us (95%)
  between operations  0.64 us (4%)
    pallas_call x1, Pallas kernels, gather_rows(): pl.pallas_call(functools.partial(gather_kernel, shares, halves), out_shap...  10.8 us
    pallas_call x1, Pallas kernels, whole_crop(): pl.pallas_call(crop_kernel, out_shape=(jax.ShapeDtypeStruct(pair_first.sh...  3.38 us

profile of v5, /device:TPU:0, one launch (start us, length us, event | category | flops | bytes accessed | tf_op | source)
XLA Modules:
  0.0 14.8 jit_solution(8338058104904695751)
XLA Ops:
  0.6 10.8 %shard_map.111 = (bf16[8,2,3,1,16,128]{5,4,3,2,1,0:T(8,128)(2,1)S(1)}, f32[2,128]{1,0:T(2,128)S(1)}, bf16[2,128,512]{2,1,0:T(8,128)(2,1)S(1)}, bf16[2,128,128]{2...) custom-call(bf16[2,16,128]{2,1,0:T(8,128)(2,1)} %first_ref.1, ...), custom_call_target="tpu_custom_call" | custom-call | tf_op jit(solution)/shard_map/pallas_call | solution.py:334
  11.4 3.4 %shard_map.112 = (bf16[2,16,128]{2,1,0:T(8,128)(2,1)}, f32[2,128,512]{2,1,0:T(8,128)}, f32[2,128,128]{2,1,0:T(8,128)}, f32[2,128,128]{2,1,0:T(8,128)}) custom-call(bf16[8,2,3,1,16,128]{5,4,3,2,1,0:T(8,128)(2,1)S(1)} %get-tuple-element.10.held, f32[2,128]{1,0:T(2,128)S(1)} %get-tuple-element.11.gain_ref, bf16[2,128,512]{2,1,0:T(8,128)(2,1)S(1)} %get-tuple-element.12.proj_ref, ...), custom_call_target="tpu_custom_call" | custom-call | tf_op jit(solution)/shard_map/pallas_call | solution.py:520
